TPU v7x, 32 devices: a whole 2x2x4 slice. The times are simulated.
32 devices in a mesh: tm: 16 (over z, x, core), mp: 2 (over y).
Axes of the slice: x: 2, y: 2, z: 4, core: 2. Of those that a mesh axis runs over, the one named last changes fastest.
Arguments:
- tokens: bfloat16 [4096, 1024], P('tm'), may hold values from -9 to 9
- norm1_gain: float32 [1024], replicated, may hold values from 0.5 to 1.5
- query_weight: bfloat16 [1024, 1024], P(None, 'mp'), may hold values from -1 to 1
- key_weight: bfloat16 [1024, 1024], P(None, 'mp'), may hold values from -1 to 1
- value_weight: bfloat16 [1024, 1024], P(None, 'mp'), may hold values from -0.1875 to 0.1875
- output_weight: bfloat16 [1024, 1024], P('mp'), may hold values from -5 to 5
- pattern: int32 [32, 8], replicated, may hold values from -1 to 31, as said below
- adjacency: int32 [128, 128], replicated, may hold values 0 or 1
- decay_rate: float32 [1024], P('mp'), may hold values from 0.015625 to 0.1
- norm2_gain: float32 [1024], replicated, may hold values from 0.5 to 1.5
- up_weight: bfloat16 [1024, 4096], P(None, 'mp'), may hold values from -0.1875 to 0.1875
- down_weight: bfloat16 [4096, 1024], P('mp'), may hold values from -0.09375 to 0.09375
Outputs:
- layer_out: bfloat16 [4096, 1024], P('tm', 'mp')
Inputs may be any that keep to these rules, and one draw needn't show every extreme that they name: pattern[b, 0] = b and pattern[b, 1] = b - 1. For the rows of the blocks g * 2 to g * 2 + 1, entry 2 + k (k from 0 to 5) is the same in all these rows: -1 where g < 2^k, else one of the blocks (g - 2^k) * 2 to (g - 2^k) * 2 + 1, never the block g * 2 - 1.
All inputs are finite; a program needn't handle non-finite values.
Results may differ from a plain program's by a relative error of at most 0.01.
Values may be sent and summed in bfloat16 or wider, within the bound.
A program may use at most 64 MiB of HBM per device.

v0:
```python
import math
import jax
import jax.numpy as jnp
from jax import lax
from jax.sharding import PartitionSpec as P

HD = 128


def from_behind(value, axis, steps):
    count = lax.axis_size(axis)
    first, last = (max(0, -steps), min(count, count - steps))
    return lax.ppermute(value, axis, [(source, source + steps) for source in range(first, last)])


def rms_norm(rows, gain):
    widened = rows.astype(jnp.float32)
    square = jnp.mean(widened * widened, axis=-1, keepdims=True)
    return (widened * lax.rsqrt(square + 1e-05) * gain).astype(jnp.bfloat16)


def block_partial(queries, key_rows, value_rows, heads):
    head_size = queries.shape[-1] // heads
    query_split = queries.reshape(queries.shape[:-1] + (heads, head_size))
    key_split = key_rows.reshape(key_rows.shape[:-1] + (heads, head_size))
    value_split = value_rows.reshape(value_rows.shape[:-1] + (heads, head_size))
    scores = jnp.einsum(
        "...qhd,...khd->...hqk", query_split, key_split, preferred_element_type=jnp.float32
    ) * (1.0 / math.sqrt(head_size))
    tops = jnp.max(scores, axis=-1)
    probs = jnp.exp(scores - tops[..., None])
    totals = jnp.sum(probs, axis=-1)
    weights = probs.astype(jnp.bfloat16)
    outputs = jnp.einsum(
        "...hqk,...khd->...qhd", weights, value_split, preferred_element_type=jnp.float32
    )
    return (tops, totals, outputs.reshape(outputs.shape[:-2] + (heads * head_size,)))


def merge_partials(tops, totals, outputs, valid, heads):
    flags = valid[..., None, None]
    masked = jnp.where(flags, tops, -jnp.inf)
    largest = jnp.max(masked, axis=-3)
    factor = jnp.where(flags, jnp.exp(jnp.where(flags, tops, 0.0) - largest[..., None, :, :]), 0.0)
    denom = jnp.sum(factor * totals, axis=-3)
    split = outputs.reshape(outputs.shape[:-1] + (heads, -1))
    numer = jnp.sum(jnp.swapaxes(factor, -1, -2)[..., None] * split, axis=-4)
    result = numer / jnp.swapaxes(denom, -1, -2)[..., None]
    return result.reshape(result.shape[:-2] + (-1,)).astype(jnp.bfloat16)


def running(frames, retain, inject):
    driven = frames.astype(jnp.float32) * inject
    factors = jnp.broadcast_to(retain, driven.shape)

    def join(earlier, later):
        return (earlier[0] * later[0], later[0] * earlier[1] + later[1])

    return lax.associative_scan(join, (factors, driven), axis=0)[1]


def per_device(
    tokens,
    norm1_gain,
    query_weight,
    key_weight,
    value_weight,
    output_weight,
    pattern,
    adjacency,
    decay_rate,
    norm2_gain,
    up_weight,
    down_weight,
):
    groups = lax.axis_size("tm")
    position = lax.axis_index("tm")
    width = query_weight.shape[1]
    heads = width // HD
    sites = adjacency.shape[0]
    steps = tokens.shape[0] // sites
    normed = rms_norm(tokens, norm1_gain)
    queries = (
        jnp.dot(normed, query_weight, preferred_element_type=jnp.float32)
        .astype(jnp.bfloat16)
        .reshape(steps, sites, width)
    )
    key_rows = jnp.dot(normed, key_weight, preferred_element_type=jnp.float32).astype(jnp.bfloat16)
    value_rows = jnp.dot(normed, value_weight, preferred_element_type=jnp.float32).astype(
        jnp.bfloat16
    )
    key_blocks = key_rows.reshape(steps, sites, width)
    value_blocks = value_rows.reshape(steps, sites, width)
    own_entries = lax.dynamic_slice_in_dim(pattern, position * steps, steps, 0)
    remote = own_entries[:, 2:]
    far_count = remote.shape[1]
    key_last, value_last = from_behind((key_blocks[steps - 1], value_blocks[steps - 1]), "tm", 1)
    prior_keys = jnp.concatenate([key_last[None], key_blocks[:-1]], axis=0)
    prior_values = jnp.concatenate([value_last[None], value_blocks[:-1]], axis=0)
    self_part = block_partial(queries, key_blocks, value_blocks, heads)
    prior_part = block_partial(queries, prior_keys, prior_values, heads)
    spread_queries = jnp.broadcast_to(queries[:, None], (steps, far_count, sites, width))
    wanted = pattern[:, 2:].reshape(groups, -1)
    local_pick = wanted - position * steps
    hits = (wanted >= 0) & (local_pick >= 0) & (local_pick < steps)
    selector = jnp.any(
        (local_pick[:, :, None] == jnp.arange(steps, dtype=jnp.int32)[None, None, :])
        & hits[:, :, None],
        axis=1,
    ).astype(jnp.bfloat16)
    send_keys = jnp.einsum(
        "gs,sbf->gbf", selector, key_blocks, preferred_element_type=jnp.float32
    ).astype(jnp.bfloat16)
    send_values = jnp.einsum(
        "gs,sbf->gbf", selector, value_blocks, preferred_element_type=jnp.float32
    ).astype(jnp.bfloat16)
    got_keys, got_values = (
        lax.all_to_all(send_keys, "tm", split_axis=0, concat_axis=0, tiled=True),
        lax.all_to_all(send_values, "tm", split_axis=0, concat_axis=0, tiled=True),
    )
    source = jnp.maximum(remote, 0) // steps
    far_part = block_partial(spread_queries, got_keys[source], got_values[source], heads)
    tops = jnp.concatenate([self_part[0][:, None], prior_part[0][:, None], far_part[0]], axis=1)
    totals = jnp.concatenate([self_part[1][:, None], prior_part[1][:, None], far_part[1]], axis=1)
    outputs = jnp.concatenate([self_part[2][:, None], prior_part[2][:, None], far_part[2]], axis=1)
    block_ids = position * steps + jnp.arange(steps, dtype=jnp.int32)
    valid = jnp.concatenate(
        [jnp.ones((steps, 1), bool), (block_ids > 0)[:, None], remote >= 0], axis=1
    )
    attended = merge_partials(tops, totals, outputs, valid, heads).reshape(steps * sites, width)
    projected = lax.psum_scatter(
        jnp.dot(attended, output_weight, preferred_element_type=jnp.float32),
        "mp",
        scatter_dimension=1,
        tiled=True,
    )
    columns = projected.shape[1]
    own_tokens = lax.dynamic_slice_in_dim(tokens, lax.axis_index("mp") * columns, columns, 1)
    first = (own_tokens.astype(jnp.float32) + projected).astype(jnp.bfloat16)
    links = jnp.maximum(adjacency, jnp.eye(sites, dtype=jnp.int32))
    degree = jnp.sum(links, axis=1).astype(jnp.float32)
    grid = first.reshape(steps, sites, columns)
    mixed = (
        jnp.einsum(
            "st,btc->bsc", links.astype(jnp.bfloat16), grid, preferred_element_type=jnp.float32
        )
        / degree[None, :, None]
    ).astype(jnp.bfloat16)
    retain = jnp.exp(-decay_rate)
    inject = jnp.sqrt(1.0 - retain * retain)
    by_site = lax.all_to_all(mixed, "tm", split_axis=1, concat_axis=0, tiled=True)
    states = running(by_site, retain, inject).astype(jnp.bfloat16)
    smoothed = lax.all_to_all(states, "tm", split_axis=0, concat_axis=1, tiled=True)
    second = (
        first.astype(jnp.float32) + smoothed.reshape(steps * sites, columns).astype(jnp.float32)
    ).astype(jnp.bfloat16)
    whole = lax.all_gather(second, "mp", axis=1, tiled=True)
    normed_late = rms_norm(whole, norm2_gain)
    hidden = jax.nn.gelu(
        jnp.dot(normed_late, up_weight, preferred_element_type=jnp.float32), approximate=True
    ).astype(jnp.bfloat16)
    summed = lax.psum_scatter(
        jnp.dot(hidden, down_weight, preferred_element_type=jnp.float32),
        "mp",
        scatter_dimension=1,
        tiled=True,
    )
    return (second.astype(jnp.float32) + summed).astype(jnp.bfloat16)


def solution(mesh):
    placed = (
        P("tm", None),
        P(),
        P(None, "mp"),
        P(None, "mp"),
        P(None, "mp"),
        P("mp", None),
        P(),
        P(),
        P("mp"),
        P(),
        P(None, "mp"),
        P("mp", None),
    )
    return jax.shard_map(
        per_device, mesh=mesh, in_specs=placed, out_specs=P("tm", "mp"), check_vma=False
    )
```

profile of v0, /device:TPU:0, one launch (start us, length us, event | category | flops | bytes accessed | tf_op | source)
XLA Modules:
  0.0 243.4 jit_solution(6739945608081619143)
XLA Ops:
  6.5 1.3 fusion.16
  7.9 0.7 slice_compare_fusion
  8.6 0.7 slice_subtract_fusion
  9.4 0.1 copy.136
  9.6 0.1 fusion.75
  9.7 1.9 convolution_convert_fusion.2
  11.6 0.8 convolution_convert_fusion
  12.4 2.5 %copy.148 = bf16[16,128,512]{2,1,0:T(8,128)(2,1)} copy(bf16[16,128,512]{2,0,1:T(8,128)(2,1)S(1)} %convolution_convert_fusion) | data formatting | bytes 4194304 | tf_op jit(solution)/shard_map/convert_element_type | solution.py:116
  15.0 7.5 %all-to-all-start.1 = ((bf16[16,128,512]{2,1,0:T(8,128)(2,1)}), bf16[16,128,512]{2,1,0:T(8,128)(2,1)S(1)}, u32[]{:S(2)}, u32[]{:S(2)}) async-start(bf16[16,128,512]{2,1,0:T(8,128)(2,1)} %copy.148), calls=%async_computation.1 | async-start | bytes 4194304 | tf_op jit(solution)/shard_map/all_to_all | solution.py:119
  22.5 1.9 convolution_convert_fusion.3
  24.4 0.7 copy-done.2
  25.1 0.8 convolution_convert_fusion.1
  25.9 2.5 %copy.138 = bf16[16,128,512]{2,1,0:T(8,128)(2,1)} copy(bf16[16,128,512]{2,0,1:T(8,128)(2,1)S(1)} %convolution_convert_fusion.1) | data formatting | bytes 4194304 | tf_op jit(solution)/shard_map/convert_element_type | solution.py:113
  28.3 35.2 %all-to-all-done.1 = bf16[16,128,512]{2,1,0:T(8,128)(2,1)S(1)} async-done(((bf16[16,128,512]{2,1,0:T(8,128)(2,1)}), bf16[16,128,512]{2,1,0:T(8,128)(2,1)S(1)}, u32[]{:S(2)}, u32[]{:S(2)}) %all-to-all-start.1) | async-done | bytes 2097184 | tf_op jit(solution)/shard_map/all_to_all | solution.py:119
  63.6 11.3 %all-to-all-start = ((bf16[16,128,512]{2,1,0:T(8,128)(2,1)}), bf16[16,128,512]{2,1,0:T(8,128)(2,1)}, u32[]{:S(2)}, u32[]{:S(2)}) async-start(bf16[16,128,512]{2,1,0:T(8,128)(2,1)} %copy.138), calls=%async_computation | async-start | bytes 4194304 | tf_op jit(solution)/shard_map/all_to_all | solution.py:118
  74.9 1.7 fusion.94
  76.6 2.9 %collective-permute-start = (bf16[128,512]{1,0:T(8,128)(2,1)}, bf16[128,512]{1,0:T(8,128)(2,1)}, u32[]{:S(2)}, u32[]{:S(2)}) collective-permute-start(bf16[128,512]{1,0:T(8,128)(2,1)} %get-tuple-element.7), channel_id=1, source_target_pairs={{0,2},{2,4},{4,6},{6,8},{8,10},{10,12},{12,14},{14,16},{16,18},{18... | collective-permute-start | bytes 393224 | tf_op jit(solution)/shard_map/ppermute | solution.py:13
  79.5 0.7 fusion.93
  80.2 3.5 %collective-permute-start.1 = (bf16[128,512]{1,0:T(8,128)(2,1)}, bf16[128,512]{1,0:T(8,128)(2,1)}, u32[]{:S(2)}, u32[]{:S(2)}) collective-permute-start(bf16[128,512]{1,0:T(8,128)(2,1)} %get-tuple-element.5), channel_id=1, source_target_pairs={{0,2},{2,4},{4,6},{6,8},{8,10},{10,12},{12,14},{14,16},{16,18},{18... | collective-permute-start | bytes 393224 | tf_op jit(solution)/shard_map/ppermute | solution.py:13
  83.8 1.7 reshape_reshape.11
  85.5 0.8 reshape_reshape.12
  86.5 2.6 %convolution_convert_fusion.4 = bf16[256,512]{1,0:T(8,128)(2,1)} fusion(bf16[1024,512]{1,0:T(8,128)(2,1)} %param.14, bf16[256,1024]{1,0:T(8,128)(2,1)} %param.12, f32[1024]{0:T(1024)S(1)} %copy-done.11, f32[256]{0:T(256)S(1)} %add_rsqrt_fusion.1), kind=kOutput, calls=%fused_computation.34 | convolution fusion | flops 269615104 | bytes 1840128 | tf_op jit(solution)/shard_map/dot_general | solution.py:84
  89.1 1.0 reshape_reshape.10
  90.1 0.7 copy.129
  90.8 0.9 concatenate.47
  91.8 0.7 copy.132
  92.4 1.0 copy.165
  93.6 0.6 copy.128
  94.2 1.3 fusion.97
  95.4 2.0 convolution_bitcast_fusion.2
  97.6 1.6 concatenate.46
  99.2 1.6 copy.131
  100.7 1.7 copy.164
  102.4 1.3 fusion.96
  103.8 2.0 convolution_bitcast_fusion.1
  105.7 1.9 gather_fusion.1
  107.6 2.6 %copy.149 = bf16[12,128,512]{1,2,0:T(8,128)(2,1)} copy(bf16[12,128,512]{2,1,0:T(8,128)(2,1)} %gather_fusion.1) | data formatting | bytes 3145728 | tf_op jit(solution)/shard_map/gather | solution.py:122
  110.2 5.8 %all-to-all-done = bf16[16,128,512]{2,1,0:T(8,128)(2,1)} async-done(((bf16[16,128,512]{2,1,0:T(8,128)(2,1)}), bf16[16,128,512]{2,1,0:T(8,128)(2,1)}, u32[]{:S(2)}, u32[]{:S(2)}) %all-to-all-start) | async-done | bytes 2097184 | tf_op jit(solution)/shard_map/all_to_all | solution.py:118
  116.0 3.4 %gather_fusion = bf16[12,128,512]{2,1,0:T(8,128)(2,1)} fusion(bf16[16,128,512]{2,1,0:T(8,128)(2,1)} %all-to-all-done, s32[1024]{0:T(1024)S(1)} %pad_clamp_fusion), kind=kCustom, calls=%fused_computation | custom fusion | bytes 3145776 | tf_op jit(solution)/shard_map/gather | solution.py:122
  119.4 1.9 copy.140
  121.4 1.3 multiply_reduce_fusion
  122.7 0.7 fusion.1
  123.4 0.7 copy-done.1
  124.1 0.7 convolution_bitcast_fusion
  125.0 0.1 copy-done.3
  125.1 0.2 copy-done.4
  125.3 0.5 fusion
  125.9 0.2 copy.153
  126.1 1.4 fusion.47
  127.6 0.1 fusion.64
  127.7 40.5 %reduce-scatter.3.cloned.1.call-done = f32[256,512]{1,0:T(8,128)} async-done(((f32[256,1024]{1,0:T(8,128)}), f32[256,512]{1,0:T(8,128)}) %reduce-scatter.3.cloned.1.call-update) | async-done | bytes 524304 | tf_op jit(solution)/shard_map/reduce_scatter | solution.py:131
  168.2 1.1 add_convert_fusion.2
  169.3 0.3 fusion.15
  169.6 0.9 copy.155
  170.5 5.6 %all-to-all-start.2 = ((bf16[2,128,512]{2,0,1:T(2,128)(2,1)}), bf16[2,128,512]{2,0,1:T(2,128)(2,1)S(1)}, u32[]{:S(2)}, u32[]{:S(2)}) async-start(bf16[2,128,512]{2,0,1:T(2,128)(2,1)} %copy.155), calls=%async_computation.3 | async-start | bytes 524288 | tf_op jit(solution)/shard_map/all_to_all | solution.py:151
  176.1 10.0 %all-to-all-done.2 = bf16[2,128,512]{2,0,1:T(2,128)(2,1)S(1)} async-done(((bf16[2,128,512]{2,0,1:T(2,128)(2,1)}), bf16[2,128,512]{2,0,1:T(2,128)(2,1)S(1)}, u32[]{:S(2)}, u32[]{:S(2)}) %all-to-all-start.2) | async-done | bytes 262176 | tf_op jit(solution)/shard_map/all_to_all | solution.py:151
  187.1 0.1 pad.39
  187.2 0.1 pad.40
  187.5 12.8 %all_to_all.28 = bf16[32,8,512]{2,1,0:T(8,128)(2,1)S(1)} all-to-all(bf16[32,8,512]{2,1,0:T(8,128)(2,1)S(1)} %add_convert_fusion.1), channel_id=1, replica_groups=mesh['tm'=16,'mp'=2] {'tm'}, dimensions={0} | all-to-all | bytes 524288 | tf_op jit(solution)/shard_map/all_to_all | solution.py:153
  200.5 8.7 %all_gather.3 = bf16[256,1024]{1,0:T(8,128)(2,1)S(1)} all-gather(bf16[256,512]{1,0:T(8,128)(2,1)S(1)} %fusion.36), channel_id=1, replica_groups=mesh['tm'=16,'mp'=2] {'mp'}, dimensions={1}, use_global_device_ids=true | all-gather | bytes 786432 | tf_op jit(solution)/shard_map/all_gather | solution.py:157
  209.3 0.2 fusion.19
  209.5 7.1 %fusion.22 = f32[256,1024]{1,0:T(8,128)} fusion(bf16[2048,1024]{1,0:T(8,128)(2,1)} %param.23, bf16[1024,2048]{1,0:T(8,128)(2,1)} %param.22, bf16[256,1024]{1,0:T(8,128)(2,1)S(1)} %all_gather.3, f32[1024]{0:T(1024)S(1)} %copy-done.12, f32[256]{0:T(256)S(1)} %add_rsqrt_fusion), kind=kOutput, calls=%fused_computation.42 | convolution fusion | flops 2153250816 | bytes 9966592 | tf_op jit(solution)/shard_map/dot_general | solution.py:163
  216.6 18.1 %reduce-scatter.5.cloned.1.call-done = f32[256,512]{1,0:T(8,128)} async-done(((f32[256,1024]{1,0:T(8,128)}), f32[256,512]{1,0:T(8,128)}) %reduce-scatter.5.cloned.1.call-update) | async-done | bytes 524304 | tf_op jit(solution)/shard_map/reduce_scatter | solution.py:162
  234.8 1.8 add_convert_fusion
  (83 shorter events, 2.3 us)
Async XLA Ops:
  6.5 119.5 %copy-start = (bf16[512,1024]{1,0:T(8,128)(2,1)S(1)}, bf16[512,1024]{1,0:T(8,128)(2,1)}, u32[]{:S(2)}) copy-start(bf16[512,1024]{1,0:T(8,128)(2,1)} %param.17) | copy-start | bytes 3145732
  15.0 7.5 %copy-start.11 = (f32[1024]{0:T(1024)S(1)}, f32[1024]{0:T(1024)}, u32[]{:S(2)}) copy-start(f32[1024]{0:T(1024)} %param.13) | copy-start | bytes 12292
  15.0 48.6 %all-to-all-start.1 = ((bf16[16,128,512]{2,1,0:T(8,128)(2,1)}), bf16[16,128,512]{2,1,0:T(8,128)(2,1)S(1)}, u32[]{:S(2)}, u32[]{:S(2)}) async-start(bf16[16,128,512]{2,1,0:T(8,128)(2,1)} %copy.148), calls=%async_computation.1 | async-start | bytes 4194304 | tf_op jit(solution)/shard_map/all_to_all | solution.py:119
  24.4 0.7 copy-start.2
  63.6 52.4 %all-to-all-start = ((bf16[16,128,512]{2,1,0:T(8,128)(2,1)}), bf16[16,128,512]{2,1,0:T(8,128)(2,1)}, u32[]{:S(2)}, u32[]{:S(2)}) async-start(bf16[16,128,512]{2,1,0:T(8,128)(2,1)} %copy.138), calls=%async_computation | async-start | bytes 4194304 | tf_op jit(solution)/shard_map/all_to_all | solution.py:118
  74.8 11.4 %copy-start.8 = (s32[32,8]{0,1:T(8,128)S(1)}, s32[32,8]{0,1:T(8,128)}, u32[]{:S(2)}) copy-start(s32[32,8]{0,1:T(8,128)} %param.18) | copy-start | bytes 3076
  74.9 93.3 %reduce-scatter.3.cloned.1.call-start = ((), (), s32[]{:S(2)}) async-start(), calls=%async_computation.6 | async-start | bytes 1572864 | tf_op jit(solution)/shard_map/reduce_scatter | solution.py:131
  76.6 21.0 %collective-permute-start = (bf16[128,512]{1,0:T(8,128)(2,1)}, bf16[128,512]{1,0:T(8,128)(2,1)}, u32[]{:S(2)}, u32[]{:S(2)}) collective-permute-start(bf16[128,512]{1,0:T(8,128)(2,1)} %get-tuple-element.7), channel_id=1, source_target_pairs={{0,2},{2,4},{4,6},{6,8},{8,10},{10,12},{12,14},{14,16},{16,18},{18... | collective-permute-start | bytes 393224 | tf_op jit(solution)/shard_map/ppermute | solution.py:13
  80.2 20.5 %collective-permute-start.1 = (bf16[128,512]{1,0:T(8,128)(2,1)}, bf16[128,512]{1,0:T(8,128)(2,1)}, u32[]{:S(2)}, u32[]{:S(2)}) collective-permute-start(bf16[128,512]{1,0:T(8,128)(2,1)} %get-tuple-element.5), channel_id=1, source_target_pairs={{0,2},{2,4},{4,6},{6,8},{8,10},{10,12},{12,14},{14,16},{16,18},{18... | collective-permute-start | bytes 393224 | tf_op jit(solution)/shard_map/ppermute | solution.py:13
  119.4 2.0 copy-start.6
  122.7 1.4 copy-start.1
  124.1 0.7 copy-start.9
  124.1 1.0 copy-start.3
  124.1 1.2 copy-start.4
  125.8 1.7 copy-start.7
  125.9 42.3 %copy-start.5 = (bf16[256,1024]{1,0:T(8,128)(2,1)S(1)}, bf16[256,1024]{1,0:T(8,128)(2,1)}, u32[]{:S(2)}) copy-start(bf16[256,1024]{1,0:T(8,128)(2,1)} %param.12) | copy-start | bytes 1572868
  127.5 48.6 %copy-start.10 = (f32[512]{0:T(512)S(1)}, f32[512]{0:T(512)}, u32[]{:S(2)}) copy-start(f32[512]{0:T(512)} %param.20) | copy-start | bytes 6148
  170.5 15.7 %all-to-all-start.2 = ((bf16[2,128,512]{2,0,1:T(2,128)(2,1)}), bf16[2,128,512]{2,0,1:T(2,128)(2,1)S(1)}, u32[]{:S(2)}, u32[]{:S(2)}) async-start(bf16[2,128,512]{2,0,1:T(2,128)(2,1)} %copy.155), calls=%async_computation.3 | async-start | bytes 524288 | tf_op jit(solution)/shard_map/all_to_all | solution.py:151
  176.1 58.7 %reduce-scatter.5.cloned.1.call-start = ((), (), s32[]{:S(2)}) async-start(), calls=%async_computation.7 | async-start | bytes 1572864 | tf_op jit(solution)/shard_map/reduce_scatter | solution.py:162
  200.3 9.1 %copy-start.12 = (f32[1024]{0:T(1024)S(1)}, f32[1024]{0:T(1024)}, u32[]{:S(2)}) copy-start(f32[1024]{0:T(1024)} %param.21) | copy-start | bytes 12292
Sparse Core Ops, SparseCore 0:
  127.7 40.4 reduce-scatter.2
  216.7 17.9 reduce-scatter.4
where the time goes:
time: 244 us; the launch traced here: 243 us
  waiting for transfers between devices  110 us (45%)
  local copies, waits for them, and re-layouts  33.6 us (14%)
  starting transfers between devices  30.9 us (13%)
  matrix products  25.2 us (10%)
  blocking collectives  21.6 us (9%)
  between operations  14 us (6%)
  other arithmetic  8.48 us (3%)
    reduce_scatter x1, waiting for transfers between devices, per_device(): lax.psum_scatter(jnp.dot(attended, output_weight, preferred_element_type=...  40.5 us
    all_to_all x1, waiting for transfers between devices, per_device(): lax.all_to_all(send_values, 'tm', split_axis=0, concat_axis=0, tiled=True)  35.2 us
    reduce_scatter x1, waiting for transfers between devices, per_device(): lax.psum_scatter(jnp.dot(hidden, down_weight, preferred_element_type=jnp....  18.1 us
    all_to_all x1, blocking collectives, per_device(): lax.all_to_all(states, 'tm', split_axis=0, concat_axis=1, tiled=True)  12.8 us
    all_to_all x1, starting transfers between devices, per_device(): lax.all_to_all(send_keys, 'tm', split_axis=0, concat_axis=0, tiled=True)  11.3 us
    all_to_all x1, waiting for transfers between devices, per_device(): lax.all_to_all(mixed, 'tm', split_axis=1, concat_axis=0, tiled=True)  9.97 us
    all_gather x1, blocking collectives, per_device(): whole = lax.all_gather(second, 'mp', axis=1, tiled=True)  8.75 us
    all_to_all x1, starting transfers between devices, per_device(): lax.all_to_all(send_values, 'tm', split_axis=0, concat_axis=0, tiled=True)  7.49 us
  transfers between devices with their start and end apart: 7, of which 5 were waited for; matrix products, arithmetic and copies ran while one was open for 14% of the time, Pallas kernels for 0%

commit v1 on v0

--- a/solution.py
+++ b/solution.py
@@ -5,6 +5,18 @@
 from jax.sharding import PartitionSpec as P
 
 HD = 128
+
+
+def exchange_directly(value, axis, split, join):
+    ways, here = (lax.axis_size(axis), lax.axis_index(axis))
+    width = value.shape[split] // ways
+    turned = jnp.roll(value, -here * width, axis=split)
+    got = [lax.slice_in_dim(turned, 0, width, axis=split)]
+    for far in range(1, ways):
+        sent = lax.slice_in_dim(turned, far * width, (far + 1) * width, axis=split)
+        got.append(lax.ppermute(sent, axis, [(d, (d + far) % ways) for d in range(ways)]))
+    line = jnp.concatenate(got[::-1], axis=join)
+    return jnp.roll(line, (here + 1) * got[0].shape[join], axis=join)
 
 
 def from_behind(value, axis, steps):
@@ -150,7 +162,7 @@
     inject = jnp.sqrt(1.0 - retain * retain)
     by_site = lax.all_to_all(mixed, "tm", split_axis=1, concat_axis=0, tiled=True)
     states = running(by_site, retain, inject).astype(jnp.bfloat16)
-    smoothed = lax.all_to_all(states, "tm", split_axis=0, concat_axis=1, tiled=True)
+    smoothed = exchange_directly(states, "tm", 0, 1)
     second = (
         first.astype(jnp.float32) + smoothed.reshape(steps * sites, columns).astype(jnp.float32)
     ).astype(jnp.bfloat16)

time: 244 us -> 255 us (1.045)
  starting transfers between devices: 30.9 us -> 49.7 us
  blocking collectives: 21.6 us -> 7.27 us
  waiting for transfers between devices: 110 us -> 115 us
    ppermute x0 -> x15, starting transfers between devices: none -> 18.8 us  [exchange_directly(): lax.ppermute(sent, axis, [(d, (d + far) % ways) for d in range(ways)])]
    all_to_all x1 -> x0, blocking collectives: 12.8 us -> none  [per_device(): lax.all_to_all(states, 'tm', split_axis=0, concat_axis=1, tiled=True)]
    ppermute x0 -> x15, waiting for transfers between devices: none -> 5.83 us  [exchange_directly(): lax.ppermute(sent, axis, [(d, (d + far) % ways) for d in range(ways)])]
  transfers between devices with their start and end apart: 7 -> 22, of which waited for: 5 -> 8; matrix products, arithmetic and copies ran while one was open for 14% -> 13% of each run, Pallas kernels for 0% -> 0%
where the time goes in v1:
time: 255 us; the launch traced here: 254 us
  waiting for transfers between devices  115 us (45%)
  starting transfers between devices  49.7 us (19%)
  local copies, waits for them, and re-layouts  33.8 us (13%)
  matrix products  25.2 us (10%)
  between operations  14.2 us (6%)
  other arithmetic  8.69 us (3%)
  blocking collectives  7.27 us (3%)
    reduce_scatter x1, waiting for transfers between devices, per_device(): lax.psum_scatter(jnp.dot(attended, output_weight, preferred_element_type=...  40.5 us
    all_to_all x1, waiting for transfers between devices, per_device(): lax.all_to_all(send_values, 'tm', split_axis=0, concat_axis=0, tiled=True)  35.2 us
    ppermute x15, starting transfers between devices, exchange_directly(): lax.ppermute(sent, axis, [(d, (d + far) % ways) for d in range(ways)])  18.8 us
    reduce_scatter x1, waiting for transfers between devices, per_device(): lax.psum_scatter(jnp.dot(hidden, down_weight, preferred_element_type=jnp....  17.9 us
    all_to_all x1, starting transfers between devices, per_device(): lax.all_to_all(send_keys, 'tm', split_axis=0, concat_axis=0, tiled=True)  11.3 us
    all_to_all x1, waiting for transfers between devices, per_device(): lax.all_to_all(mixed, 'tm', split_axis=1, concat_axis=0, tiled=True)  9.94 us
    all_to_all x1, starting transfers between devices, per_device(): lax.all_to_all(send_values, 'tm', split_axis=0, concat_axis=0, tiled=True)  7.49 us
    all_gather x1, blocking collectives, per_device(): whole = lax.all_gather(second, 'mp', axis=1, tiled=True)  7.27 us
  transfers between devices with their start and end apart: 22, of which 8 were waited for; matrix products, arithmetic and copies ran while one was open for 13% of the time, Pallas kernels for 0%

profile of v1, /device:TPU:0, one launch (start us, length us, event | category | flops | bytes accessed | tf_op | source)
XLA Modules:
  0.0 253.9 jit_solution(1273020102757085261)
XLA Ops:
  6.5 1.3 fusion.16
  7.9 0.7 slice_compare_fusion
  8.6 0.7 slice_subtract_fusion
  9.7 1.9 convolution_convert_fusion.2
  11.6 0.8 convolution_convert_fusion
  12.4 2.5 copy.175
  15.0 7.5 %all-to-all-start.1 = ((bf16[16,128,512]{2,1,0:T(8,128)(2,1)}), bf16[16,128,512]{2,1,0:T(8,128)(2,1)S(1)}, u32[]{:S(2)}, u32[]{:S(2)}) async-start(bf16[16,128,512]{2,1,0:T(8,128)(2,1)} %copy.175), calls=%async_computation.1 | async-start | bytes 4194304 | tf_op jit(solution)/shard_map/all_to_all | solution.py:131
  22.5 1.9 convolution_convert_fusion.3
  24.4 0.7 copy-done.2
  25.1 0.8 convolution_convert_fusion.1
  25.9 2.5 copy.165
  28.3 35.2 %all-to-all-done.1 = bf16[16,128,512]{2,1,0:T(8,128)(2,1)S(1)} async-done(((bf16[16,128,512]{2,1,0:T(8,128)(2,1)}), bf16[16,128,512]{2,1,0:T(8,128)(2,1)S(1)}, u32[]{:S(2)}, u32[]{:S(2)}) %all-to-all-start.1) | async-done | bytes 2097184 | tf_op jit(solution)/shard_map/all_to_all | solution.py:131
  63.6 11.3 %all-to-all-start = ((bf16[16,128,512]{2,1,0:T(8,128)(2,1)}), bf16[16,128,512]{2,1,0:T(8,128)(2,1)}, u32[]{:S(2)}, u32[]{:S(2)}) async-start(bf16[16,128,512]{2,1,0:T(8,128)(2,1)} %copy.165), calls=%async_computation | async-start | bytes 4194304 | tf_op jit(solution)/shard_map/all_to_all | solution.py:130
  74.9 1.7 fusion.96
  76.6 2.9 %collective-permute-start = (bf16[128,512]{1,0:T(8,128)(2,1)}, bf16[128,512]{1,0:T(8,128)(2,1)}, u32[]{:S(2)}, u32[]{:S(2)}) collective-permute-start(bf16[128,512]{1,0:T(8,128)(2,1)} %get-tuple-element.22), channel_id=1, source_target_pairs={{0,2},{2,4},{4,6},{6,8},{8,10},{10,12},{12,14},{14,16},{16,18},{18... | collective-permute-start | bytes 393224 | tf_op jit(solution)/shard_map/ppermute | solution.py:25
  79.5 0.7 fusion.95
  80.2 3.5 %collective-permute-start.1 = (bf16[128,512]{1,0:T(8,128)(2,1)}, bf16[128,512]{1,0:T(8,128)(2,1)}, u32[]{:S(2)}, u32[]{:S(2)}) collective-permute-start(bf16[128,512]{1,0:T(8,128)(2,1)} %get-tuple-element.20), channel_id=1, source_target_pairs={{0,2},{2,4},{4,6},{6,8},{8,10},{10,12},{12,14},{14,16},{16,18},{18... | collective-permute-start | bytes 393224 | tf_op jit(solution)/shard_map/ppermute | solution.py:25
  83.8 1.7 reshape_reshape.11
  85.5 0.8 reshape_reshape.12
  86.5 2.6 %convolution_convert_fusion.4 = bf16[256,512]{1,0:T(8,128)(2,1)} fusion(bf16[1024,512]{1,0:T(8,128)(2,1)} %param.14, bf16[256,1024]{1,0:T(8,128)(2,1)} %param.12, f32[1024]{0:T(1024)S(1)} %copy-done.11, f32[256]{0:T(256)S(1)} %add_rsqrt_fusion.1), kind=kOutput, calls=%fused_computation.34 | convolution fusion | flops 269615104 | bytes 1840128 | tf_op jit(solution)/shard_map/dot_general | solution.py:96
  89.1 1.0 reshape_reshape.10
  90.1 0.7 copy.156
  90.9 0.9 concatenate.57
  91.8 0.7 copy.159
  92.5 1.0 copy.191
  94.3 1.3 fusion.99
  95.5 2.0 convolution_bitcast_fusion.2
  97.7 1.6 concatenate.56
  99.2 1.6 copy.158
  100.8 1.7 copy.190
  102.5 1.3 fusion.98
  103.9 2.0 convolution_bitcast_fusion.1
  105.8 1.9 gather_fusion.1
  107.7 2.6 %copy.176 = bf16[12,128,512]{1,2,0:T(8,128)(2,1)} copy(bf16[12,128,512]{2,1,0:T(8,128)(2,1)} %gather_fusion.1) | data formatting | bytes 3145728 | tf_op jit(solution)/shard_map/gather | solution.py:134
  110.3 5.7 %all-to-all-done = bf16[16,128,512]{2,1,0:T(8,128)(2,1)} async-done(((bf16[16,128,512]{2,1,0:T(8,128)(2,1)}), bf16[16,128,512]{2,1,0:T(8,128)(2,1)}, u32[]{:S(2)}, u32[]{:S(2)}) %all-to-all-start) | async-done | bytes 2097184 | tf_op jit(solution)/shard_map/all_to_all | solution.py:130
  116.0 3.4 %gather_fusion = bf16[12,128,512]{2,1,0:T(8,128)(2,1)} fusion(bf16[16,128,512]{2,1,0:T(8,128)(2,1)} %all-to-all-done, s32[1024]{0:T(1024)S(1)} %pad_clamp_fusion), kind=kCustom, calls=%fused_computation | custom fusion | bytes 3145776 | tf_op jit(solution)/shard_map/gather | solution.py:134
  119.4 1.9 copy.167
  121.4 1.3 multiply_reduce_fusion
  122.7 0.7 fusion.1
  123.4 0.7 copy-done.1
  124.1 0.7 convolution_bitcast_fusion
  126.1 1.4 fusion.48
  127.7 40.5 %reduce-scatter.3.cloned.1.call-done = f32[256,512]{1,0:T(8,128)} async-done(((f32[256,1024]{1,0:T(8,128)}), f32[256,512]{1,0:T(8,128)}) %reduce-scatter.3.cloned.1.call-update) | async-done | bytes 524304 | tf_op jit(solution)/shard_map/reduce_scatter | solution.py:143
  168.1 1.1 add_convert_fusion.2
  169.5 0.9 copy.182
  170.4 5.6 %all-to-all-start.2 = ((bf16[2,128,512]{2,0,1:T(2,128)(2,1)}), bf16[2,128,512]{2,0,1:T(2,128)(2,1)S(1)}, u32[]{:S(2)}, u32[]{:S(2)}) async-start(bf16[2,128,512]{2,0,1:T(2,128)(2,1)} %copy.182), calls=%async_computation.3 | async-start | bytes 524288 | tf_op jit(solution)/shard_map/all_to_all | solution.py:163
  176.1 9.9 %all-to-all-done.2 = bf16[2,128,512]{2,0,1:T(2,128)(2,1)S(1)} async-done(((bf16[2,128,512]{2,0,1:T(2,128)(2,1)}), bf16[2,128,512]{2,0,1:T(2,128)(2,1)S(1)}, u32[]{:S(2)}, u32[]{:S(2)}) %all-to-all-start.2) | async-done | bytes 262176 | tf_op jit(solution)/shard_map/all_to_all | solution.py:163
  187.7 1.4 collective-permute-start.2
  189.2 1.0 collective-permute-start.3
  190.2 0.9 collective-permute-start.5
  191.1 2.0 collective-permute-start.6
  193.1 1.6 collective-permute-start.7
  195.0 2.1 collective-permute-start.9
  197.1 2.3 collective-permute-start.10
  199.4 1.5 collective-permute-start.11
  201.0 2.2 collective-permute-start.13
  203.3 2.1 collective-permute-start.14
  205.3 1.2 collective-permute-start.15
  206.6 1.8 collective-permute-done.14
  208.5 3.3 %collective-permute-done.15 = bf16[2,8,512]{2,1,0:T(8,128)(2,1)S(1)} collective-permute-done((bf16[2,8,512]{2,1,0:T(8,128)(2,1)S(1)}, bf16[2,8,512]{2,1,0:T(8,128)(2,1)S(1)}, u32[]{:S(2)}, u32[]{:S(2)}) %collective-permute-start.15) | collective-permute-done | bytes 16416 | tf_op jit(solution)/shard_map/ppermute | solution.py:17
  212.7 7.3 %all_gather.3 = bf16[256,1024]{1,0:T(8,128)(2,1)S(1)} all-gather(bf16[256,512]{1,0:T(8,128)(2,1)S(1)} %fusion.36), channel_id=1, replica_groups=mesh['tm'=16,'mp'=2] {'mp'}, dimensions={1}, use_global_device_ids=true | all-gather | bytes 786432 | tf_op jit(solution)/shard_map/all_gather | solution.py:169
  220.2 7.1 %fusion.22 = f32[256,1024]{1,0:T(8,128)} fusion(bf16[2048,1024]{1,0:T(8,128)(2,1)} %param.23, bf16[1024,2048]{1,0:T(8,128)(2,1)} %param.22, bf16[256,1024]{1,0:T(8,128)(2,1)S(1)} %all_gather.3, f32[1024]{0:T(1024)S(1)} %copy-done.12, f32[256]{0:T(256)S(1)} %add_rsqrt_fusion), kind=kOutput, calls=%fused_computation.42 | convolution fusion | flops 2153250816 | bytes 9966592 | tf_op jit(solution)/shard_map/dot_general | solution.py:175
  227.3 17.9 %reduce-scatter.5.cloned.1.call-done = f32[256,512]{1,0:T(8,128)} async-done(((f32[256,1024]{1,0:T(8,128)}), f32[256,512]{1,0:T(8,128)}) %reduce-scatter.5.cloned.1.call-update) | async-done | bytes 524304 | tf_op jit(solution)/shard_map/reduce_scatter | solution.py:174
  245.3 1.8 add_convert_fusion
  (145 shorter events, 6.4 us)
Async XLA Ops:
  6.5 119.5 %copy-start = (bf16[512,1024]{1,0:T(8,128)(2,1)S(1)}, bf16[512,1024]{1,0:T(8,128)(2,1)}, u32[]{:S(2)}) copy-start(bf16[512,1024]{1,0:T(8,128)(2,1)} %param.17) | copy-start | bytes 3145732
  15.0 7.5 %copy-start.11 = (f32[1024]{0:T(1024)S(1)}, f32[1024]{0:T(1024)}, u32[]{:S(2)}) copy-start(f32[1024]{0:T(1024)} %param.13) | copy-start | bytes 12292
  15.0 48.6 %all-to-all-start.1 = ((bf16[16,128,512]{2,1,0:T(8,128)(2,1)}), bf16[16,128,512]{2,1,0:T(8,128)(2,1)S(1)}, u32[]{:S(2)}, u32[]{:S(2)}) async-start(bf16[16,128,512]{2,1,0:T(8,128)(2,1)} %copy.175), calls=%async_computation.1 | async-start | bytes 4194304 | tf_op jit(solution)/shard_map/all_to_all | solution.py:131
  24.4 0.7 copy-start.2
  63.6 52.4 %all-to-all-start = ((bf16[16,128,512]{2,1,0:T(8,128)(2,1)}), bf16[16,128,512]{2,1,0:T(8,128)(2,1)}, u32[]{:S(2)}, u32[]{:S(2)}) async-start(bf16[16,128,512]{2,1,0:T(8,128)(2,1)} %copy.165), calls=%async_computation | async-start | bytes 4194304 | tf_op jit(solution)/shard_map/all_to_all | solution.py:130
  74.8 11.4 %copy-start.8 = (s32[32,8]{0,1:T(8,128)S(1)}, s32[32,8]{0,1:T(8,128)}, u32[]{:S(2)}) copy-start(s32[32,8]{0,1:T(8,128)} %param.18) | copy-start | bytes 3076
  74.8 93.3 %reduce-scatter.3.cloned.1.call-start = ((), (), s32[]{:S(2)}) async-start(), calls=%async_computation.5 | async-start | bytes 1572864 | tf_op jit(solution)/shard_map/reduce_scatter | solution.py:143
  76.6 21.1 %collective-permute-start = (bf16[128,512]{1,0:T(8,128)(2,1)}, bf16[128,512]{1,0:T(8,128)(2,1)}, u32[]{:S(2)}, u32[]{:S(2)}) collective-permute-start(bf16[128,512]{1,0:T(8,128)(2,1)} %get-tuple-element.22), channel_id=1, source_target_pairs={{0,2},{2,4},{4,6},{6,8},{8,10},{10,12},{12,14},{14,16},{16,18},{18... | collective-permute-start | bytes 393224 | tf_op jit(solution)/shard_map/ppermute | solution.py:25
  80.2 20.6 %collective-permute-start.1 = (bf16[128,512]{1,0:T(8,128)(2,1)}, bf16[128,512]{1,0:T(8,128)(2,1)}, u32[]{:S(2)}, u32[]{:S(2)}) collective-permute-start(bf16[128,512]{1,0:T(8,128)(2,1)} %get-tuple-element.20), channel_id=1, source_target_pairs={{0,2},{2,4},{4,6},{6,8},{8,10},{10,12},{12,14},{14,16},{16,18},{18... | collective-permute-start | bytes 393224 | tf_op jit(solution)/shard_map/ppermute | solution.py:25
  119.4 2.0 copy-start.6
  122.7 1.4 copy-start.1
  124.1 0.7 copy-start.9
  124.1 1.0 copy-start.3
  124.1 1.2 copy-start.4
  125.8 1.7 copy-start.7
  125.8 42.3 %copy-start.5 = (bf16[256,1024]{1,0:T(8,128)(2,1)S(1)}, bf16[256,1024]{1,0:T(8,128)(2,1)}, u32[]{:S(2)}) copy-start(bf16[256,1024]{1,0:T(8,128)(2,1)} %param.12) | copy-start | bytes 1572868
  127.5 48.6 %copy-start.10 = (f32[512]{0:T(512)S(1)}, f32[512]{0:T(512)}, u32[]{:S(2)}) copy-start(f32[512]{0:T(512)} %param.20) | copy-start | bytes 6148
  170.4 15.7 %all-to-all-start.2 = ((bf16[2,128,512]{2,0,1:T(2,128)(2,1)}), bf16[2,128,512]{2,0,1:T(2,128)(2,1)S(1)}, u32[]{:S(2)}, u32[]{:S(2)}) async-start(bf16[2,128,512]{2,0,1:T(2,128)(2,1)} %copy.182), calls=%async_computation.3 | async-start | bytes 524288 | tf_op jit(solution)/shard_map/all_to_all | solution.py:163
  176.0 69.3 %reduce-scatter.5.cloned.1.call-start = ((), (), s32[]{:S(2)}) async-start(), calls=%async_computation.6 | async-start | bytes 1572864 | tf_op jit(solution)/shard_map/reduce_scatter | solution.py:174
  187.7 32.5 %copy-start.12 = (f32[1024]{0:T(1024)S(1)}, f32[1024]{0:T(1024)}, u32[]{:S(2)}) copy-start(f32[1024]{0:T(1024)} %param.21) | copy-start | bytes 12292
  187.7 5.4 %collective-permute-start.2 = (bf16[2,8,512]{2,1,0:T(8,128)(2,1)S(1)}, bf16[2,8,512]{2,1,0:T(8,128)(2,1)S(1)}, u32[]{:S(2)}, u32[]{:S(2)}) collective-permute-start(bf16[2,8,512]{2,1,0:T(8,128)(2,1)S(1)} %get-tuple-element.19), channel_id=1, source_target_pairs={{0,30},{2,0},{4,2},{6,4},{8,6},{10,8},{12,10},{14,12},{16,14},{18,... | collective-permute-start | bytes 49160 | tf_op jit(solution)/shard_map/ppermute | solution.py:17
  189.2 5.6 %collective-permute-start.3 = (bf16[2,8,512]{2,1,0:T(8,128)(2,1)S(1)}, bf16[2,8,512]{2,1,0:T(8,128)(2,1)S(1)}, u32[]{:S(2)}, u32[]{:S(2)}) collective-permute-start(bf16[2,8,512]{2,1,0:T(8,128)(2,1)S(1)} %get-tuple-element.18), channel_id=1, source_target_pairs={{0,28},{2,30},{4,0},{6,2},{8,4},{10,6},{12,8},{14,10},{16,12},{18,... | collective-permute-start | bytes 49160 | tf_op jit(solution)/shard_map/ppermute | solution.py:17
  190.2 4.8 %collective-permute-start.4 = (bf16[2,8,512]{2,1,0:T(8,128)(2,1)S(1)}, bf16[2,8,512]{2,1,0:T(8,128)(2,1)S(1)}, u32[]{:S(2)}, u32[]{:S(2)}) collective-permute-start(bf16[2,8,512]{2,1,0:T(8,128)(2,1)S(1)} %get-tuple-element.17), channel_id=1, source_target_pairs={{0,26},{2,28},{4,30},{6,0},{8,2},{10,4},{12,6},{14,8},{16,10},{18,... | collective-permute-start | bytes 49160 | tf_op jit(solution)/shard_map/ppermute | solution.py:17
  190.2 6.9 %collective-permute-start.5 = (bf16[2,8,512]{2,1,0:T(8,128)(2,1)S(1)}, bf16[2,8,512]{2,1,0:T(8,128)(2,1)S(1)}, u32[]{:S(2)}, u32[]{:S(2)}) collective-permute-start(bf16[2,8,512]{2,1,0:T(8,128)(2,1)S(1)} %get-tuple-element.16), channel_id=1, source_target_pairs={{0,24},{2,26},{4,28},{6,30},{8,0},{10,2},{12,4},{14,6},{16,8},{18,... | collective-permute-start | bytes 49160 | tf_op jit(solution)/shard_map/ppermute | solution.py:17
  191.1 8.3 %collective-permute-start.6 = (bf16[2,8,512]{2,1,0:T(8,128)(2,1)S(1)}, bf16[2,8,512]{2,1,0:T(8,128)(2,1)S(1)}, u32[]{:S(2)}, u32[]{:S(2)}) collective-permute-start(bf16[2,8,512]{2,1,0:T(8,128)(2,1)S(1)} %get-tuple-element.15), channel_id=1, source_target_pairs={{0,22},{2,24},{4,26},{6,28},{8,30},{10,0},{12,2},{14,4},{16,6},{18... | collective-permute-start | bytes 49160 | tf_op jit(solution)/shard_map/ppermute | solution.py:17
  193.1 7.9 %collective-permute-start.7 = (bf16[2,8,512]{2,1,0:T(8,128)(2,1)S(1)}, bf16[2,8,512]{2,1,0:T(8,128)(2,1)S(1)}, u32[]{:S(2)}, u32[]{:S(2)}) collective-permute-start(bf16[2,8,512]{2,1,0:T(8,128)(2,1)S(1)} %get-tuple-element.14), channel_id=1, source_target_pairs={{0,20},{2,22},{4,24},{6,26},{8,28},{10,30},{12,0},{14,2},{16,4},{1... | collective-permute-start | bytes 49160 | tf_op jit(solution)/shard_map/ppermute | solution.py:17
  194.7 6.3 %collective-permute-start.8 = (bf16[2,8,512]{2,1,0:T(8,128)(2,1)S(1)}, bf16[2,8,512]{2,1,0:T(8,128)(2,1)S(1)}, u32[]{:S(2)}, u32[]{:S(2)}) collective-permute-start(bf16[2,8,512]{2,1,0:T(8,128)(2,1)S(1)} %get-tuple-element.13), channel_id=1, source_target_pairs={{0,18},{2,20},{4,22},{6,24},{8,26},{10,28},{12,30},{14,0},{16,2},{... | collective-permute-start | bytes 49160 | tf_op jit(solution)/shard_map/ppermute | solution.py:17
  195.0 8.2 %collective-permute-start.9 = (bf16[2,8,512]{2,1,0:T(8,128)(2,1)S(1)}, bf16[2,8,512]{2,1,0:T(8,128)(2,1)S(1)}, u32[]{:S(2)}, u32[]{:S(2)}) collective-permute-start(bf16[2,8,512]{2,1,0:T(8,128)(2,1)S(1)} %get-tuple-element.12), channel_id=1, source_target_pairs={{0,16},{2,18},{4,20},{6,22},{8,24},{10,26},{12,28},{14,30},{16,0},... | collective-permute-start | bytes 49160 | tf_op jit(solution)/shard_map/ppermute | solution.py:17
  197.1 8.2 %collective-permute-start.10 = (bf16[2,8,512]{2,1,0:T(8,128)(2,1)S(1)}, bf16[2,8,512]{2,1,0:T(8,128)(2,1)S(1)}, u32[]{:S(2)}, u32[]{:S(2)}) collective-permute-start(bf16[2,8,512]{2,1,0:T(8,128)(2,1)S(1)} %get-tuple-element.11), channel_id=1, source_target_pairs={{0,14},{2,16},{4,18},{6,20},{8,22},{10,24},{12,26},{14,28},{16,30}... | collective-permute-start | bytes 49160 | tf_op jit(solution)/shard_map/ppermute | solution.py:17
  199.4 7.1 %collective-permute-start.11 = (bf16[2,8,512]{2,1,0:T(8,128)(2,1)S(1)}, bf16[2,8,512]{2,1,0:T(8,128)(2,1)S(1)}, u32[]{:S(2)}, u32[]{:S(2)}) collective-permute-start(bf16[2,8,512]{2,1,0:T(8,128)(2,1)S(1)} %get-tuple-element.10), channel_id=1, source_target_pairs={{0,12},{2,14},{4,16},{6,18},{8,20},{10,22},{12,24},{14,26},{16,28}... | collective-permute-start | bytes 49160 | tf_op jit(solution)/shard_map/ppermute | solution.py:17
  201.0 5.6 %collective-permute-start.12 = (bf16[2,8,512]{2,1,0:T(8,128)(2,1)S(1)}, bf16[2,8,512]{2,1,0:T(8,128)(2,1)S(1)}, u32[]{:S(2)}, u32[]{:S(2)}) collective-permute-start(bf16[2,8,512]{2,1,0:T(8,128)(2,1)S(1)} %get-tuple-element.9), channel_id=1, source_target_pairs={{0,10},{2,12},{4,14},{6,16},{8,18},{10,20},{12,22},{14,24},{16,26}... | collective-permute-start | bytes 49160 | tf_op jit(solution)/shard_map/ppermute | solution.py:17
  201.0 5.6 %collective-permute-start.13 = (bf16[2,8,512]{2,1,0:T(8,128)(2,1)S(1)}, bf16[2,8,512]{2,1,0:T(8,128)(2,1)S(1)}, u32[]{:S(2)}, u32[]{:S(2)}) collective-permute-start(bf16[2,8,512]{2,1,0:T(8,128)(2,1)S(1)} %get-tuple-element.8), channel_id=1, source_target_pairs={{0,8},{2,10},{4,12},{6,14},{8,16},{10,18},{12,20},{14,22},{16,24},... | collective-permute-start | bytes 49160 | tf_op jit(solution)/shard_map/ppermute | solution.py:17
  203.3 5.2 %collective-permute-start.14 = (bf16[2,8,512]{2,1,0:T(8,128)(2,1)S(1)}, bf16[2,8,512]{2,1,0:T(8,128)(2,1)S(1)}, u32[]{:S(2)}, u32[]{:S(2)}) collective-permute-start(bf16[2,8,512]{2,1,0:T(8,128)(2,1)S(1)} %get-tuple-element.7), channel_id=1, source_target_pairs={{0,6},{2,8},{4,10},{6,12},{8,14},{10,16},{12,18},{14,20},{16,22},{... | collective-permute-start | bytes 49160 | tf_op jit(solution)/shard_map/ppermute | solution.py:17
  205.3 6.4 %collective-permute-start.15 = (bf16[2,8,512]{2,1,0:T(8,128)(2,1)S(1)}, bf16[2,8,512]{2,1,0:T(8,128)(2,1)S(1)}, u32[]{:S(2)}, u32[]{:S(2)}) collective-permute-start(bf16[2,8,512]{2,1,0:T(8,128)(2,1)S(1)} %get-tuple-element.6), channel_id=1, source_target_pairs={{0,4},{2,6},{4,8},{6,10},{8,12},{10,14},{12,16},{14,18},{16,20},{1... | collective-permute-start | bytes 49160 | tf_op jit(solution)/shard_map/ppermute | solution.py:17
  206.6 5.9 %collective-permute-start.16 = (bf16[2,8,512]{2,1,0:T(8,128)(2,1)S(1)}, bf16[2,8,512]{2,1,0:T(8,128)(2,1)S(1)}, u32[]{:S(2)}, u32[]{:S(2)}) collective-permute-start(bf16[2,8,512]{2,1,0:T(8,128)(2,1)S(1)} %get-tuple-element.5), channel_id=1, source_target_pairs={{0,2},{2,4},{4,6},{6,8},{8,10},{10,12},{12,14},{14,16},{16,18},{18... | collective-permute-start | bytes 49160 | tf_op jit(solution)/shard_map/ppermute | solution.py:17
Sparse Core Ops, SparseCore 0:
  127.6 40.4 reduce-scatter.2
  227.5 17.7 reduce-scatter.4
